TPU v7x, 512 devices: a whole 4x4x16 slice. The times are simulated.
512 devices in a mesh: wide: 64 (over z, y_hi, core), narrow: 8 (over x, y_lo).
Axes of the slice: x: 4, y: 4 (y_hi: 2, y_lo: 2; y = y_hi * 2 + y_lo), z: 16, core: 2. Of those that a mesh axis runs over, the one named last changes fastest.
Arguments:
- points: float32 [32, 98304], P(None, ('wide', 'narrow')), may hold values from -6 to 6
- lengthscale: float32 [32], replicated, may hold values from 2.5 to 8
- noise: float32 [1], replicated, may hold values from 1 to 16
- direction: float32 [32, 98304], P(None, ('wide', 'narrow')), may hold values from -10.8 to 10.8
- residual: float32 [32, 98304], P(None, ('wide', 'narrow')), may hold values from -10.8 to 10.8
- solution: float32 [32, 98304], P(None, ('wide', 'narrow')), may hold values from -6 to 6
Outputs:
- new_solution: float32 [32, 98304], P(None, ('wide', 'narrow'))
- new_residual: float32 [32, 98304], P(None, ('wide', 'narrow'))
- new_direction: float32 [32, 98304], P(None, ('wide', 'narrow'))
- norm_sq: float32 [32], replicated
All inputs are finite; a program needn't handle non-finite values.
Results may differ from a plain program's by a relative error of at most 0.0024.
Values may be sent and summed in bfloat16 or wider, within the bound.
A program may use at most 64 MiB of HBM per device.

v0:
```python
import math

import jax
import jax.numpy as jnp
from jax import lax
from jax.sharding import PartitionSpec as P


def kernel_tile(home_s, home_n, vis_s):
    cross = lax.dot_general(
        home_s,
        vis_s,
        (((0,), (0,)), ((), ())),
        precision=lax.Precision.HIGHEST,
        preferred_element_type=jnp.float32,
    )
    vis_n = jnp.sum(vis_s * vis_s, axis=0)
    dist_sq = home_n[:, None] + vis_n[None, :] - 2.0 * cross
    radius = jnp.sqrt(5.0 * jnp.maximum(dist_sq, 0.0))
    return ((1.0 + radius + radius * radius / 3.0) * jnp.exp(-radius)).astype(jnp.bfloat16)


def forward(tile, dirs_bf):
    return lax.dot_general(
        dirs_bf, tile, (((1,), (1,)), ((), ())), preferred_element_type=jnp.float32
    )


def body(points, lengthscale, noise, direction, residual, solution):
    scale_col = lengthscale[:, None]
    home_pts = lax.all_gather(points, "narrow", axis=1, tiled=True)
    home_s = home_pts / scale_col
    home_n = jnp.sum(home_s * home_s, axis=0)
    empty = jnp.zeros((direction.shape[0], home_s.shape[1]), jnp.float32)
    pts = lax.all_gather(points, "wide", axis=1, tiled=True)
    dirs = lax.all_gather(direction, "wide", axis=1, tiled=True)
    width = pts.shape[1]
    block = math.gcd(width, 512)
    count = width // block
    pts_blocks = pts.reshape(pts.shape[0], count, block).transpose(1, 0, 2)
    dir_blocks = dirs.reshape(dirs.shape[0], count, block).transpose(1, 0, 2)

    def one_block(acc, item):
        tile = kernel_tile(home_s, home_n, item[0] / scale_col)
        return (acc + forward(tile, item[1].astype(jnp.bfloat16)), None)

    total = lax.scan(one_block, empty, (pts_blocks, dir_blocks))[0]
    kernel_dir = lax.psum_scatter(total, "narrow", scatter_dimension=1, tiled=True)
    kernel_dir = kernel_dir + noise[0] * direction
    resid_sq = lax.psum(jnp.sum(residual * residual, axis=1), ("wide", "narrow"))
    curve = lax.psum(jnp.sum(direction * kernel_dir, axis=1), ("wide", "narrow"))
    alpha = resid_sq / curve
    new_residual = residual - alpha[:, None] * kernel_dir
    norm_sq = lax.psum(jnp.sum(new_residual * new_residual, axis=1), ("wide", "narrow"))
    new_solution = solution + alpha[:, None] * direction
    new_direction = new_residual + (norm_sq / resid_sq)[:, None] * direction
    return (new_solution, new_residual, new_direction, norm_sq)


def solution(mesh):
    return jax.shard_map(
        body,
        mesh=mesh,
        in_specs=(
            P(None, ("wide", "narrow")),
            P(),
            P(),
            P(None, ("wide", "narrow")),
            P(None, ("wide", "narrow")),
            P(None, ("wide", "narrow")),
        ),
        out_specs=(
            P(None, ("wide", "narrow")),
            P(None, ("wide", "narrow")),
            P(None, ("wide", "narrow")),
            P(),
        ),
        check_vma=False,
    )
```

profile of v0, /device:TPU:1, one launch (start us, length us, event | category | flops | bytes accessed | tf_op | source)
XLA Modules:
  0.0 595.8 jit_solution(5864830892474288)
XLA Ops:
  8.0 23.3 %all-gather.1 = f32[8,192,32]{1,2,0:T(8,128)S(1)} all-gather(f32[1,192,32]{1,2,0:T(8,128)} %bitcast.77), channel_id=1, replica_groups=mesh['wide'=64,'narrow'=8] {'narrow'}, dimensions={0}, use_global_device_ids=true | all-gather | bytes 221184 | tf_op jit(solution)/shard_map/all_gather | solution.py:31
  32.3 93.6 %all-gather = bf16[64,192,32]{1,2,0:T(8,128)(2,1)S(1)} all-gather(bf16[1,192,32]{1,2,0:T(8,128)(2,1)S(1)} %bitcast_convert_fusion), channel_id=1, replica_groups=mesh['wide'=64,'narrow'=8] {'wide'}, dimensions={0}, use_global_device_ids=true | all-gather | bytes 798720 | tf_op jit(solution)/shard_map/all_gather | solution.py:36
  126.4 1.1 reshape.23
  127.6 1.2 copy.29
  129.5 32.4 %all-gather.5.cloned.1.call-done = f32[64,192,32]{1,2,0:T(8,128)} async-done(((f32[1,192,32]{1,2,0:T(8,128)}), f32[64,192,32]{1,2,0:T(8,128)}) %all-gather.5.cloned.1.call-update) | async-done | bytes 1572880 | tf_op jit(solution)/shard_map/all_gather | solution.py:35
  161.9 2.8 copy.22
  164.7 2.0 reshape.27
  166.7 2.3 copy.30
  169.0 173.7 %while.11 = (s32[]{:T(128)}, f32[32,1536]{1,0:T(8,128)S(1)}, bf16[24,32,512]{2,0,1:T(8,128)(2,1)}, f32[1536]{0:T(1024)S(1)}, f32[24,32,512]{2,0,1:T(8,128)S(1)},...) while((s32[]{:T(128)}, f32[32,1536]{1,0:T(8,128)S(1)}, ...), condition=%wide.region_5.6_spmd.clone, body=%wide.region_3.0_spmd.clone.sunk | while | flops 361922048 | bytes 4106607 | solution.py:47
  169.2 5.6 multiply_convert_fusion.2
  174.8 1.0 constant_dynamic-slice_fusion.5
  176.4 5.6 multiply_convert_fusion.2
  182.1 1.0 constant_dynamic-slice_fusion.5
  183.7 5.6 multiply_convert_fusion.2
  189.3 1.0 constant_dynamic-slice_fusion.5
  190.9 5.6 multiply_convert_fusion.2
  196.5 1.0 constant_dynamic-slice_fusion.5
  198.1 5.6 multiply_convert_fusion.2
  203.8 1.0 constant_dynamic-slice_fusion.5
  205.4 5.6 multiply_convert_fusion.2
  211.0 1.0 constant_dynamic-slice_fusion.5
  212.6 5.6 multiply_convert_fusion.2
  218.3 1.0 constant_dynamic-slice_fusion.5
  219.9 5.6 multiply_convert_fusion.2
  225.5 1.0 constant_dynamic-slice_fusion.5
  227.1 5.6 multiply_convert_fusion.2
  232.7 1.0 constant_dynamic-slice_fusion.5
  234.3 5.6 multiply_convert_fusion.2
  240.0 1.0 constant_dynamic-slice_fusion.5
  241.6 5.6 multiply_convert_fusion.2
  247.2 1.0 constant_dynamic-slice_fusion.5
  248.8 5.6 multiply_convert_fusion.2
  256.0 5.6 multiply_convert_fusion.2
  263.3 5.6 multiply_convert_fusion.2
  270.5 5.6 multiply_convert_fusion.2
  277.7 5.6 multiply_convert_fusion.2
  285.0 5.6 multiply_convert_fusion.2
  292.2 5.6 multiply_convert_fusion.2
  299.4 5.6 multiply_convert_fusion.2
  306.7 5.6 multiply_convert_fusion.2
  313.9 5.6 multiply_convert_fusion.2
  321.2 5.6 multiply_convert_fusion.2
  328.4 5.6 multiply_convert_fusion.2
  335.6 5.6 multiply_convert_fusion.2
  342.7 1.2 copy.25
  344.5 34.5 %reduce-scatter.4.cloned.1.call-done = f32[192,32]{1,0:T(8,128)} async-done(((f32[1536,32]{1,0:T(8,128)}), f32[192,32]{1,0:T(8,128)}) %reduce-scatter.4.cloned.1.call-update) | async-done | bytes 24592
  380.1 106.9 %all-reduce = (f32[32]{0:T(128)S(1)}, f32[32]{0:T(128)S(1)}) all-reduce(f32[32]{0:T(128)S(1)} %get-tuple-element.109, f32[32]{0:T(128)S(1)} %get-tuple-element.108), channel_id=1, replica_groups=mesh['wide'=64,'narrow'=8] {'wide','narrow'}, use_global_device_ids=true, to_apply=%region_1.2 | all-reduce | flops 64 | bytes 512 | tf_op jit(solution)/shard_map/psum | solution.py:50
  487.8 100.5 %psum.23 = f32[32]{0:T(128)S(1)} all-reduce(f32[32]{0:T(128)S(1)} %get-tuple-element.103), channel_id=1, replica_groups=mesh['wide'=64,'narrow'=8] {'wide','narrow'}, use_global_device_ids=true, to_apply=%region_10.11 | all-reduce | flops 32 | bytes 256 | tf_op jit(solution)/shard_map/psum | solution.py:54
  (113 shorter events, 32.0 us)
Async XLA Ops:
  7.2 154.7 %all-gather.5.cloned.1.call-start = ((), (), s32[]{:S(2)}) async-start(), calls=%async_computation.1 | async-start | bytes 2129920 | tf_op jit(solution)/shard_map/all_gather | solution.py:35
  7.9 371.1 %reduce-scatter.4.cloned.1.call-start = ((), (), s32[]{:S(2)}) async-start(), calls=%async_computation.2 | async-start | bytes 884736
  126.4 2.3 copy-start.4
  169.0 211.0 %copy-start = (f32[32,192]{1,0:T(8,128)S(1)}, f32[32,192]{1,0:T(8,128)}, u32[]{:S(2)}) copy-start(f32[32,192]{1,0:T(8,128)} %param.11) | copy-start | bytes 73732
  169.0 211.0 %copy-start.1 = (f32[32,192]{1,0:T(8,128)S(1)}, f32[32,192]{1,0:T(8,128)}, u32[]{:S(2)}) copy-start(f32[32,192]{1,0:T(8,128)} %param.12) | copy-start | bytes 73732
  169.0 318.0 %copy-start.3 = (f32[32,192]{1,0:T(8,128)S(1)}, f32[32,192]{1,0:T(8,128)}, u32[]{:S(2)}) copy-start(f32[32,192]{1,0:T(8,128)} %param.13) | copy-start | bytes 73732
  487.8 101.2 %copy-start.2 = (f32[32,192]{1,0:T(8,128)}, f32[32,192]{1,0:T(8,128)S(1)}, u32[]{:S(2)}) copy-start(f32[32,192]{1,0:T(8,128)S(1)} %get-tuple-element.104) | copy-start | bytes 73732
  588.3 0.7 copy-start.5
Sparse Core Ops, SparseCore 0:
  11.3 150.5 all-gather.4
  344.0 34.9 reduce-scatter.3
where the time goes:
time: 598 us; the launch traced here: 596 us
  blocking collectives  324 us (54%)
  matrix products  144 us (24%)
  waiting for transfers between devices  67.6 us (11%)
  local copies, waits for them, and re-layouts  38.4 us (6%)
  between operations  14.8 us (2%)
    dot_general x24, matrix products, kernel_tile(): lax.dot_general(home_s, vis_s, (((0,), (0,)), ((), ())), precision=lax.Pr...  135 us
    psum x1, blocking collectives, body(): lax.psum(jnp.sum(residual * residual, axis=1), ('wide', 'narrow'))  107 us
    psum x1, blocking collectives, body(): lax.psum(jnp.sum(new_residual * new_residual, axis=1), ('wide', 'narrow'))  100 us
    all_gather x1, blocking collectives, body(): dirs = lax.all_gather(direction, 'wide', axis=1, tiled=True)  93.6 us
    unnamed x3, waiting for transfers between devices  35.2 us
    all_gather x1, waiting for transfers between devices, body(): pts = lax.all_gather(points, 'wide', axis=1, tiled=True)  32.4 us
    dynamic_slice x48, local copies, waits for them, and re-layouts, body(): total = lax.scan(one_block, empty, (pts_blocks, dir_blocks))[0]  26.1 us
    all_gather x1, blocking collectives, body(): home_pts = lax.all_gather(points, 'narrow', axis=1, tiled=True)  23.3 us
  transfers between devices with their start and end apart: 2, of which 2 were waited for; matrix products, arithmetic and copies ran while one was open for 1% of the time, Pallas kernels for 0%

commit v1 on v0

v1 whole, which is shorter than its diff:
```python
import functools
import math

import jax
import jax.numpy as jnp
from jax import lax
from jax.experimental import pallas as pl
from jax.experimental.pallas import tpu as pltpu
from jax.sharding import PartitionSpec as P

F32, BF16 = jnp.float32, jnp.bfloat16
MESH = pl.DeviceIdType.MESH
NX, NY, NZ = 4, 4, 16
NPEER = NX * NY
BLK = 192
CHUNK = NY * BLK
HOME = NPEER * BLK
VIS = 2 * BLK
HALF = NZ // 2
COORD_SCALE = math.sqrt(5.0) / 3.0
EXP_SCALE = -3.0 * math.log2(math.e)
EXP_SHIFT = math.log2(3.0)
NT = (((1,), (1,)), ((), ()))


def matern(u):
    u = jnp.maximum(u, 1e-30)
    q = u * lax.rsqrt(u)
    e = jnp.exp2(q * EXP_SCALE + EXP_SHIFT)
    return (((u + q) + (1.0 / 3.0)) * e).astype(BF16)


def pack_tail(tail):
    lane = lax.broadcasted_iota(jnp.int32, (16, 128), 1)
    return jnp.where(lane < 64, tail[0:16], pltpu.roll(tail[16:32], 64, 1))


def unpack_tails(a, b):
    lane = lax.broadcasted_iota(jnp.int32, (16, 128), 1)
    top = jnp.where(lane < 64, a, pltpu.roll(b, 64, 1))
    bottom = jnp.where(lane < 64, pltpu.roll(a, 64, 1), b)
    return jnp.concatenate([top, bottom], axis=0)


def unpack(blocks):
    heads = [b[0:32] for b in blocks]
    tails = [unpack_tails(blocks[i][32:48], blocks[i + 1][32:48]) for i in range(0, len(blocks), 2)]
    return jnp.concatenate(heads + tails, axis=1)


def split3(v):
    hi = v.astype(BF16)
    rest = v - hi.astype(F32)
    mid = rest.astype(BF16)
    lo = (rest - mid.astype(F32)).astype(BF16)
    return hi, mid, lo


def norm_rows(s, first):
    sq = jnp.sum(s * s, axis=0, keepdims=True)
    hi, mid, lo = (p.astype(F32) for p in split3(sq))
    row = lax.broadcasted_iota(jnp.int32, (16, s.shape[1]), 0)
    ones = jnp.where(row < 6, 1.0, 0.0)
    rows = jnp.where(row == first, hi, jnp.where(row == first + 1, mid, jnp.where(row == first + 2, lo, ones)))
    return rows.astype(BF16)


def home_operand(s):
    hi, mid, lo = split3(s)
    pad = jnp.zeros((48, s.shape[1]), BF16)
    return jnp.concatenate([hi, hi, mid, mid, hi, lo, norm_rows(s, 0), pad], axis=0)


def visitor_operand(s):
    hi, mid, lo = split3(s)
    hi, mid, lo = (p * BF16(-2.0) for p in (hi, mid, lo))
    pad = jnp.zeros((48, s.shape[1]), BF16)
    return jnp.concatenate([hi, mid, hi, mid, lo, hi, norm_rows(s, 3), pad], axis=0).T


def to_row(cols):
    lane = lax.broadcasted_iota(jnp.int32, (32, 128), 1)
    sub = lax.broadcasted_iota(jnp.int32, (32, 128), 0)
    out = jnp.zeros((32, 128), F32)
    for i, col in enumerate(cols):
        out = jnp.where(lane == sub + 32 * i, col, out)
    return jnp.sum(out, axis=0, keepdims=True)


def to_col(row, i):
    lane = lax.broadcasted_iota(jnp.int32, (32, 128), 1)
    sub = lax.broadcasted_iota(jnp.int32, (32, 128), 0)
    return jnp.sum(jnp.where(lane == sub + 32 * i, row, 0.0), axis=1, keepdims=True)


def kernel(
    pts_ref, ls_ref, noise_ref, dir_ref, res_ref, sol_ref,
    sol_out, res_out, dir_out, norm_out,
    tail, own_s, own_d, home_s, home_d, vis_s, vis_d, hb, hd, va, vd, hacc, vacc,
    chain, fin_a, fin_b, red_a, red_b, ar1_src, ar1, ar2_src, ar2, ar3_src, ar3,
    home_send, home_recv, zs_send, z_recv, sib_send, sib_recv, ch_send, ch_recv,
    fin_send, fin_recv, red_send, red_recv, ar1_send, ar1_recv, ar2_send, ar2_recv, ar3_send, ar3_recv,
):
    wide, narrow = lax.axis_index("wide"), lax.axis_index("narrow")
    z, y_hi, core = wide // 4, (wide // 2) % 2, wide % 2
    x, y_lo = narrow // 2, narrow % 2
    y = y_hi * 2 + y_lo

    def peer(dz=0, dx=0, dy=0, dc=0):
        pz, px, py, pc = (z + dz) % NZ, (x + dx) % NX, (y + dy) % NY, (core + dc) % 2
        return (pz * 4 + (py // 2) * 2 + pc, px * 2 + py % 2)

    def remote(src, dst, send, recv, dev):
        return pltpu.make_async_remote_copy(
            src_ref=src, dst_ref=dst, send_sem=send, recv_sem=recv, device_id=dev, device_id_type=MESH
        )

    plane = [(dx, dy) for dx in range(NX) for dy in range(NY)]

    barrier = pltpu.get_barrier_semaphore()
    for dx, dy in plane[1:]:
        pl.semaphore_signal(barrier, inc=1, device_id=peer(dx=dx, dy=dy), device_id_type=MESH)
    for dz in range(1, NZ):
        pl.semaphore_signal(barrier, inc=1, device_id=peer(dz=dz), device_id_type=MESH)
    pl.semaphore_signal(barrier, inc=1, device_id=peer(dc=1), device_id_type=MESH)
    pl.semaphore_signal(barrier, inc=1, device_id=peer(dz=NZ - (HALF - 1), dc=1), device_id_type=MESH)

    eye = lax.broadcasted_iota(jnp.int32, (32, 32), 0) == lax.broadcasted_iota(jnp.int32, (32, 32), 1)
    scale = jnp.sum(jnp.where(eye, ls_ref[...], 0.0), axis=1, keepdims=True)
    scaled = pts_ref[...] / scale * COORD_SCALE
    own_s[0:32] = scaled[:, 0:128]
    tail[...] = jnp.zeros_like(tail)
    tail[:, 0:64] = scaled[:, 128:192]
    own_s[32:48] = pack_tail(tail[...])
    own_d[0:32] = dir_ref[:, 0:128].astype(BF16)
    tail[:, 0:64] = dir_ref[:, 128:192]
    own_d[32:48] = pack_tail(tail[...]).astype(BF16)
    hacc[...] = jnp.zeros_like(hacc)

    pl.semaphore_wait(barrier, 2 + NZ - 1 + NPEER - 1)

    def home_copy(i, which):
        dx, dy = plane[i]
        back = plane.index(((-dx) % NX, (-dy) % NY))
        src, dst = ((own_s, home_s), (own_d, home_d))[which]
        return remote(src, dst.at[back], home_send.at[which, i], home_recv.at[which, back], peer(dx=dx, dy=dy))

    def z_copy(k, which):
        src, dst = ((vis_s, vis_d))[which], ((vis_s, vis_d))[which]
        return remote(src.at[k, 0], dst.at[k + 1, 0], zs_send.at[which, k], z_recv.at[which, k + 1], peer(dz=NZ - 1))

    def sib_copy(k, which):
        buf = (vis_s, vis_d)[which]
        return remote(buf.at[k, 0], buf.at[k, 1], sib_send.at[which, k], sib_recv.at[which, k], peer(dc=1))

    vis_s[0, 0] = own_s[...]
    vis_d[0, 0] = own_d[...]
    for which in range(2):
        z_copy(0, which).start()
        sib_copy(0, which).start()
    for i in range(1, NPEER):
        for which in range(2):
            home_copy(i, which).start()

    def set_visitors(k):
        va[...] = visitor_operand(unpack([vis_s[k, 0], vis_s[k, 1]]))
        vd[...] = unpack([vis_d[k, 0].astype(F32), vis_d[k, 1].astype(F32)]).astype(BF16)

    def arrived(k):
        for which in range(2):
            z_copy(k - 1, which).wait_recv()
        for which in range(2):
            sib_copy(k, which).start()

    for which in range(2):
        sib_copy(0, which).wait_recv()
    set_visitors(0)
    home_s[0] = own_s[...]
    home_d[0] = own_d[...]
    for g in range(NX):
        for i in range(4 * g, 4 * g + 4):
            if i:
                for which in range(2):
                    home_copy(plane.index(((-plane[i][0]) % NX, (-plane[i][1]) % NY)), which).wait_recv()
        cols = pl.ds(g * CHUNK, CHUNK)
        hb[:, cols] = home_operand(unpack([home_s[i] for i in range(4 * g, 4 * g + 4)]))
        hd[:, cols] = unpack([home_d[i].astype(F32) for i in range(4 * g, 4 * g + 4)]).astype(BF16)

    def tile(cols):
        return matern(jnp.dot(va[...], hb[:, cols], preferred_element_type=F32))

    def home_only(t, carry):
        cols = pl.ds(pl.multiple_of(t * CHUNK, CHUNK), CHUNK)
        hacc[:, cols] += jnp.dot(vd[...], tile(cols), preferred_element_type=F32)
        return carry

    lax.fori_loop(0, NX, home_only, 0)

    arrived(1)
    for which in range(2):
        z_copy(1, which).start()

    def both(k, carry):
        arrived(k + 1)

        @pl.when(k < HALF - 1)
        def _():
            for which in range(2):
                z_copy(k + 1, which).start()

        for which in range(2):
            sib_copy(k, which).wait_recv()
        set_visitors(k)
        vacc[...] = jnp.zeros_like(vacc)

        def one(t, inner):
            cols = pl.ds(pl.multiple_of(t * 2 * CHUNK, 2 * CHUNK), 2 * CHUNK)
            k_tile = tile(cols)
            hacc[:, cols] += jnp.dot(vd[...], k_tile, preferred_element_type=F32)
            vacc[...] += lax.dot_general(hd[:, cols], k_tile, NT, preferred_element_type=F32)
            return inner

        lax.fori_loop(0, NX // 2, one, 0)

        @pl.when(k == 1)
        def _():
            chain[k] = vacc[...]

        @pl.when(k > 1)
        def _():
            chain_copy(k - 1).wait_recv()
            chain[k] += vacc[...]

        @pl.when(k < HALF - 1)
        def _():
            chain_copy(k).start()

        return carry

    def chain_copy(k):
        return remote(chain.at[k], chain.at[k + 1], ch_send.at[k], ch_recv.at[k + 1], peer(dz=NZ - 1))

    lax.fori_loop(1, HALF, both, 0)

    def fin_copy(f, part):
        src = chain.at[HALF - 1, :, pl.ds(128 * f, 128)] if part == 0 else chain.at[HALF - 1, :, pl.ds(256, 128)]
        dst = (fin_a, fin_b)[part].at[f]
        return remote(src, dst, fin_send.at[f, part], fin_recv.at[f, part], peer(dz=HALF - 1, dc=f))

    for f in range(2):
        for part in range(2):
            fin_copy(f, part).start()

    for which in range(2):
        sib_copy(HALF, which).wait_recv()
    set_visitors(HALF)

    def red_copy(i, part):
        dx, dy = plane[i]
        back = plane.index(((-dx) % NX, (-dy) % NY))
        base = dx * CHUNK + (128 * dy if part == 0 else 512 + 128 * (dy // 2))
        src = hacc.at[:, pl.ds(base, 128)]
        dst = (red_a, red_b)[part].at[back]
        return remote(src, dst, red_send.at[part, i], red_recv.at[part, back], peer(dx=dx, dy=dy))

    for g in (1, 2, 3, 0):
        home_only(g, 0)
        for i in range(4 * g, 4 * g + 4):
            if i:
                for part in range(2):
                    red_copy(i, part).start()

    sum_a = hacc[:, 0:128]
    even, odd = hacc[:, 512:640], jnp.zeros((32, 128), F32)
    for f in range(2):
        for part in range(2):
            fin_copy(f, part).wait_recv()
    sum_a = sum_a + fin_a[0] + fin_a[1]
    even = even + fin_b[0]
    odd = odd + fin_b[1]
    for i in range(1, NPEER):
        back = plane.index(((-plane[i][0]) % NX, (-plane[i][1]) % NY))
        for part in range(2):
            red_copy(back, part).wait_recv()
        sum_a = sum_a + red_a[i]
        if i % 2:
            odd = odd + red_b[i]
        else:
            even = even + red_b[i]
    sum_b = even[:, 0:64] + pltpu.roll(odd, 64, 1)[:, 0:64]
    direction = dir_ref[...]
    residual = res_ref[...]
    kd = jnp.concatenate([sum_a, sum_b], axis=1) + noise_ref[0] * direction

    def total(v):
        return jnp.sum(v, axis=1, keepdims=True)

    sums = to_row([total(residual * residual), total(direction * kd), total(residual * kd), total(kd * kd)])

    ar1_src[...] = jnp.broadcast_to(sums, (8, 128))
    me1 = x * NY + y

    def ar1_copy(dx, dy, slot):
        return remote(ar1_src, ar1.at[slot], ar1_send.at[dx * NY + dy], ar1_recv.at[slot], peer(dx=dx, dy=dy))

    for dx, dy in plane[1:]:
        ar1_copy(dx, dy, me1).start()
    ar1[me1] = ar1_src[...]
    for dx, dy in plane[1:]:
        ar1_copy(dx, dy, ((x + dx) % NX) * NY + (y + dy) % NY).wait_recv()
    acc = ar1[0]
    for i in range(1, NPEER):
        acc = acc + ar1[i]
    ar2_src[...] = acc

    def ar2_copy(dz, slot):
        return remote(ar2_src, ar2.at[slot], ar2_send.at[dz], ar2_recv.at[slot], peer(dz=dz))

    for dz in range(1, NZ):
        ar2_copy(dz, z).start()
    ar2[z] = acc
    for dz in range(1, NZ):
        ar2_copy(dz, (z + dz) % NZ).wait_recv()
    acc = ar2[0]
    for i in range(1, NZ):
        acc = acc + ar2[i]
    ar3_src[...] = acc
    last = remote(ar3_src, ar3, ar3_send, ar3_recv, peer(dc=1))
    last.start()
    last.wait_recv()
    acc = (ar3_src[...] + ar3[...])[0:1]

    rr, curve, r_kd, kd_sq = (to_col(acc, i) for i in range(4))
    alpha = rr / curve
    norm_sq = rr - 2.0 * alpha * r_kd + alpha * alpha * kd_sq
    new_residual = residual - alpha * kd
    sol_out[...] = sol_ref[...] + alpha * direction
    res_out[...] = new_residual
    dir_out[...] = new_residual + (norm_sq / rr) * direction
    norm_out[...] = jnp.sum(jnp.where(eye, norm_sq, 0.0), axis=0, keepdims=True)

    for which in range(2):
        for k in range(HALF):
            z_copy(k, which).wait_send()
        for k in range(HALF + 1):
            sib_copy(k, which).wait_send()
        for i in range(1, NPEER):
            home_copy(i, which).wait_send()
            red_copy(i, which).wait_send()
    for k in range(1, HALF - 1):
        chain_copy(k).wait_send()
    for f in range(2):
        for part in range(2):
            fin_copy(f, part).wait_send()
    for dx, dy in plane[1:]:
        ar1_copy(dx, dy, me1).wait_send()
    for dz in range(1, NZ):
        ar2_copy(dz, z).wait_send()
    last.wait_send()


def body(points, lengthscale, noise, direction, residual, solution):
    vmem, smem = pl.BlockSpec(memory_space=pltpu.VMEM), pl.BlockSpec(memory_space=pltpu.SMEM)
    block = jax.ShapeDtypeStruct((32, BLK), F32)
    dma = pltpu.SemaphoreType.DMA
    out = pl.pallas_call(
        kernel,
        out_shape=[block, block, block, jax.ShapeDtypeStruct((1, 32), F32)],
        in_specs=[vmem, vmem, smem, vmem, vmem, vmem],
        out_specs=[vmem] * 4,
        scratch_shapes=[
            pltpu.VMEM((32, 128), F32),
            pltpu.VMEM((48, 128), F32),
            pltpu.VMEM((48, 128), BF16),
            pltpu.VMEM((NPEER, 48, 128), F32),
            pltpu.VMEM((NPEER, 48, 128), BF16),
            pltpu.VMEM((HALF + 1, 2, 48, 128), F32),
            pltpu.VMEM((HALF + 1, 2, 48, 128), BF16),
            pltpu.VMEM((256, HOME), BF16),
            pltpu.VMEM((32, HOME), BF16),
            pltpu.VMEM((VIS, 256), BF16),
            pltpu.VMEM((32, VIS), BF16),
            pltpu.VMEM((32, HOME), F32),
            pltpu.VMEM((32, VIS), F32),
            pltpu.VMEM((HALF, 32, VIS), F32),
            pltpu.VMEM((2, 32, 128), F32),
            pltpu.VMEM((2, 32, 128), F32),
            pltpu.VMEM((NPEER, 32, 128), F32),
            pltpu.VMEM((NPEER, 32, 128), F32),
            pltpu.VMEM((8, 128), F32),
            pltpu.VMEM((NPEER, 8, 128), F32),
            pltpu.VMEM((8, 128), F32),
            pltpu.VMEM((NZ, 8, 128), F32),
            pltpu.VMEM((8, 128), F32),
            pltpu.VMEM((8, 128), F32),
            dma((2, NPEER)), dma((2, NPEER)),
            dma((2, HALF + 1)), dma((2, HALF + 1)),
            dma((2, HALF + 1)), dma((2, HALF + 1)),
            dma((HALF,)), dma((HALF,)),
            dma((2, 2)), dma((2, 2)),
            dma((2, NPEER)), dma((2, NPEER)),
            dma((NPEER,)), dma((NPEER,)),
            dma((NZ,)), dma((NZ,)),
            dma, dma,
        ],
        compiler_params=pltpu.CompilerParams(
            collective_id=0, has_side_effects=True, vmem_limit_bytes=40 * 1024 * 1024
        ),
    )(points, lengthscale.reshape(1, 32), noise, direction, residual, solution)
    return (out[0], out[1], out[2], out[3].reshape(32))


def solution(mesh):
    data = P(None, ("wide", "narrow"))
    return jax.shard_map(
        body,
        mesh=mesh,
        in_specs=(data, P(), P(), data, data, data),
        out_specs=(data, data, data, P()),
        check_vma=False,
    )
```

time: 598 us -> 92.8 us (0.16)
  blocking collectives: 324 us -> 0 us
  matrix products: 144 us -> 0 us
  Pallas kernels: 0 us -> 85.1 us
  waiting for transfers between devices: 67.6 us -> 0 us
  local copies, waits for them, and re-layouts: 38.4 us -> 6.03 us
  between operations: 14.8 us -> 1.3 us
    psum x2 -> x0, blocking collectives: 207 us -> none  [the longest x1 107 us: body(): lax.psum(jnp.sum(residual * residual, axis=1), ('wide', 'narrow'))]
    dot_general x48 -> x0, matrix products: 144 us -> none  [the longest x24 135 us: kernel_tile(): lax.dot_general(home_s, vis_s, (((0,), (0,)), ((), ())), precision=lax.Pr...]
    all_gather x2 -> x0, blocking collectives: 117 us -> none  [the longest x1 93.6 us: body(): dirs = lax.all_gather(direction, 'wide', axis=1, tiled=True)]
    pallas_call x0 -> x1, Pallas kernels: none -> 85.1 us  [body(): pl.pallas_call(kernel, out_shape=[block, block, block, jax.ShapeDtypeStru...]
    unnamed x3 -> x0, waiting for transfers between devices: 35.2 us -> none
    all_gather x1 -> x0, waiting for transfers between devices: 32.4 us -> none  [body(): pts = lax.all_gather(points, 'wide', axis=1, tiled=True)]
    dynamic_slice x48 -> x0, local copies, waits for them, and re-layouts: 26.1 us -> none  [body(): total = lax.scan(one_block, empty, (pts_blocks, dir_blocks))[0]]
  transfers between devices with their start and end apart: 2 -> 0, of which waited for: 2 -> 0; matrix products, arithmetic and copies ran while one was open for 1% -> 0% of each run, Pallas kernels for 0% -> 0%
where the time goes in v1:
time: 92.8 us; the launch traced here: 92.4 us
  Pallas kernels  85.1 us (92%)
  local copies, waits for them, and re-layouts  6.03 us (6%)
  between operations  1.3 us (1%)
    pallas_call x1, Pallas kernels, body(): pl.pallas_call(kernel, out_shape=[block, block, block, jax.ShapeDtypeStru...  85.1 us
    unnamed x14, local copies, waits for them, and re-layouts  6.03 us

profile of v1, /device:TPU:1, one launch (start us, length us, event | category | flops | bytes accessed | tf_op | source)
XLA Modules:
  0.0 92.4 jit_solution(13093748984318485028)
XLA Ops:
  1.3 0.0 copy-start.4
  1.3 0.6 copy-done.4
  1.9 0.0 copy-start
  1.9 0.8 copy-done
  2.7 0.0 copy-start.1
  2.7 0.8 copy-done.1
  3.5 0.0 copy-start.2
  3.5 0.8 copy-done.2
  4.2 0.0 copy-start.3
  4.2 0.8 copy-done.3
  5.0 85.1 %shard_map.93 = (f32[32,192]{1,0:T(8,128)S(1)}, f32[32,192]{1,0:T(8,128)S(1)}, f32[32,192]{1,0:T(8,128)S(1)}, f32[1,32]{1,0:T(1,128)S(1)}) custom-call(f32[32,192]{1,0:T(8,128)S(1)} %copy-done, f32[1,32]{1,0:T(1,128)S(1)} %bitcast.2, f32[1]{0:T(128)S(6)} %copy.14.noise_ref, f32[32,192]{1,0:T(8,128)S(1)} %copy-done.1, f32[32,192]{1,0:T(8,128)S(1)} %copy-done.2, ...), custom_call_target="tpu_custom_call" | custom-call | tf_op jit(solution)/shard_map/pallas_call | solution.py:366
  90.0 0.6 copy.15
  90.7 0.6 copy.16
  91.3 0.6 copy.17
  91.9 0.5 copy.18
Async XLA Ops:
  1.3 0.7 copy-start.4
  1.9 0.8 copy-start
  2.7 0.8 copy-start.1
  3.5 0.8 copy-start.2
  4.2 0.8 copy-start.3

commit v2 on v1

v2 whole, which is shorter than its diff:
```python
import functools
import math

import jax
import jax.numpy as jnp
from jax import lax
from jax.experimental import pallas as pl
from jax.experimental.pallas import tpu as pltpu
from jax.sharding import PartitionSpec as P

F32, BF16 = jnp.float32, jnp.bfloat16
MESH = pl.DeviceIdType.MESH
NX, NY, NZ = 4, 4, 16
NPEER = NX * NY
BLK = 192
CHUNK = NY * BLK
HOME = NPEER * BLK
VIS = 2 * BLK
HALF = NZ // 2
COORD_SCALE = math.sqrt(5.0) / 3.0
EXP_SCALE = -3.0 * math.log2(math.e)
EXP_SHIFT = math.log2(3.0)
NT = (((1,), (1,)), ((), ()))


def matern(u):
    u = jnp.maximum(u, 1e-30)
    q = u * lax.rsqrt(u)
    e = jnp.exp2(q * EXP_SCALE + EXP_SHIFT)
    return (((u + q) + (1.0 / 3.0)) * e).astype(BF16)


def pack_tail(tail):
    lane = lax.broadcasted_iota(jnp.int32, (16, 128), 1)
    return jnp.where(lane < 64, tail[0:16], pltpu.roll(tail[16:32], 64, 1))


def pack_high(tail):
    lane = lax.broadcasted_iota(jnp.int32, (16, 128), 1)
    return jnp.where(lane < 64, pltpu.roll(tail[0:16], 64, 1), tail[16:32])


def unpack_tails(a, b):
    lane = lax.broadcasted_iota(jnp.int32, (16, 128), 1)
    top = jnp.where(lane < 64, a, pltpu.roll(b, 64, 1))
    bottom = jnp.where(lane < 64, pltpu.roll(a, 64, 1), b)
    return jnp.concatenate([top, bottom], axis=0)


def unpack(blocks):
    heads = [b[0:32] for b in blocks]
    tails = [unpack_tails(blocks[i][32:48], blocks[i + 1][32:48]) for i in range(0, len(blocks), 2)]
    return jnp.concatenate(heads + tails, axis=1)


def split3(v):
    hi = v.astype(BF16)
    rest = v - hi.astype(F32)
    mid = rest.astype(BF16)
    lo = (rest - mid.astype(F32)).astype(BF16)
    return hi, mid, lo


def norm_rows(s, first):
    sq = jnp.sum(s * s, axis=0, keepdims=True)
    hi, mid, lo = (p.astype(F32) for p in split3(sq))
    row = lax.broadcasted_iota(jnp.int32, (16, s.shape[1]), 0)
    ones = jnp.where(row < 6, 1.0, 0.0)
    rows = jnp.where(row == first, hi, jnp.where(row == first + 1, mid, jnp.where(row == first + 2, lo, ones)))
    return rows.astype(BF16)


def home_operand(s):
    hi, mid, lo = split3(s)
    pad = jnp.zeros((48, s.shape[1]), BF16)
    return jnp.concatenate([hi, hi, mid, mid, hi, lo, norm_rows(s, 0), pad], axis=0)


def visitor_operand(s):
    hi, mid, lo = split3(s)
    hi, mid, lo = (p * BF16(-2.0) for p in (hi, mid, lo))
    pad = jnp.zeros((48, s.shape[1]), BF16)
    return jnp.concatenate([hi, mid, hi, mid, lo, hi, norm_rows(s, 3), pad], axis=0).T


def to_row(cols):
    lane = lax.broadcasted_iota(jnp.int32, (32, 128), 1)
    sub = lax.broadcasted_iota(jnp.int32, (32, 128), 0)
    out = jnp.zeros((32, 128), F32)
    for i, col in enumerate(cols):
        out = jnp.where(lane == sub + 32 * i, col, out)
    return jnp.sum(out, axis=0, keepdims=True)


def to_col(row, i):
    lane = lax.broadcasted_iota(jnp.int32, (32, 128), 1)
    sub = lax.broadcasted_iota(jnp.int32, (32, 128), 0)
    return jnp.sum(jnp.where(lane == sub + 32 * i, row, 0.0), axis=1, keepdims=True)


def kernel(
    pts_hbm, ls_hbm, noise_ref, dir_hbm, res_hbm,
    kd_out, coef_out,
    pts_ref, ls_ref, dir_ref, res_ref,
    tail, own_s, own_d, home_s, home_d, vis_s, vis_d, hb, hd, va, vd, hacc, ret, ret_tail, sum_head, sum_tail, red_tail,
    cross_a, cross_b, fin_a, fin_b, red_a, red_b, ar1_src, ar1, ar2_src, ar2, ar3_src, ar3,
    in_sem, home_send, home_recv, zs_send, z_recv, sib_send, sib_recv,
    cross_send, cross_recv, fin_send, fin_recv, red_send, red_recv, ar1_send, ar1_recv, ar2_send, ar2_recv, ar3_send, ar3_recv,
):
    wide, narrow = lax.axis_index("wide"), lax.axis_index("narrow")
    z, y_hi, core = wide // 4, (wide // 2) % 2, wide % 2
    x, y_lo = narrow // 2, narrow % 2
    y = y_hi * 2 + y_lo

    def peer(dz=0, dx=0, dy=0, dc=0):
        pz, px, py, pc = (z + dz) % NZ, (x + dx) % NX, (y + dy) % NY, (core + dc) % 2
        return (pz * 4 + (py // 2) * 2 + pc, px * 2 + py % 2)

    def remote(src, dst, send, recv, dev):
        return pltpu.make_async_remote_copy(
            src_ref=src, dst_ref=dst, send_sem=send, recv_sem=recv, device_id=dev, device_id_type=MESH
        )

    plane = [(dx, dy) for dx in range(NX) for dy in range(NY)]

    fetches = [
        pltpu.make_async_copy(src, dst, in_sem.at[i])
        for i, (src, dst) in enumerate(((pts_hbm, pts_ref), (ls_hbm, ls_ref), (dir_hbm, dir_ref), (res_hbm, res_ref)))
    ]
    for fetch in fetches:
        fetch.start()

    barrier = pltpu.get_barrier_semaphore()
    senders = [dict(dx=dx, dy=dy) for dx, dy in plane[1:]] + [dict(dz=1), dict(dz=2), dict(dc=1)]
    for sender in senders:
        pl.semaphore_signal(barrier, inc=1, device_id=peer(**sender), device_id_type=MESH)

    for fetch in fetches[:3]:
        fetch.wait()
    eye = lax.broadcasted_iota(jnp.int32, (32, 32), 0) == lax.broadcasted_iota(jnp.int32, (32, 32), 1)
    scale = jnp.sum(jnp.where(eye, ls_ref[...], 0.0), axis=1, keepdims=True)
    scaled = pts_ref[...] / scale * COORD_SCALE
    own_s[0:32] = scaled[:, 0:128]
    tail[...] = jnp.zeros_like(tail)
    tail[:, 0:64] = scaled[:, 128:192]
    own_s[32:48] = pack_tail(tail[...])
    own_d[0:32] = dir_ref[:, 0:128].astype(BF16)
    tail[:, 0:64] = dir_ref[:, 128:192]
    own_d[32:48] = pack_tail(tail[...]).astype(BF16)

    hacc[...] = jnp.zeros_like(hacc)
    ret[...] = jnp.zeros_like(ret)
    pl.semaphore_wait(barrier, len(senders))

    own, vis, home = (own_s, own_d), (vis_s, vis_d), (home_s, home_d)

    def home_copy(dx, dy, slot, which):
        return remote(
            own[which], home[which].at[slot], home_send.at[which, dx * NY + dy], home_recv.at[which, slot], peer(dx=dx, dy=dy)
        )

    def z_copy(k, which):
        src = own[which] if k <= 2 else vis[which].at[k - 2, 0]
        return remote(src, vis[which].at[k, 0], zs_send.at[which, k], z_recv.at[which, k], peer(dz=NZ - min(k, 2)))

    def sib_copy(k, which):
        src = own[which] if k == 0 else vis[which].at[k, 0]
        return remote(src, vis[which].at[k, 1], sib_send.at[which, k], sib_recv.at[which, k], peer(dc=1))

    def home_start(which):
        for dx, dy in plane[1:]:
            home_copy(dx, dy, ((-dx) % NX) * NY + (-dy) % NY, which).start()

    for which in range(2):
        sib_copy(0, which).start()
    for k in (1, 2):
        for which in range(2):
            z_copy(k, which).start()
    home_start(0)
    home_start(1)

    vis_s[0, 0] = own_s[...]
    vis_d[0, 0] = own_d[...]
    home_s[0] = own_s[...]
    home_d[0] = own_d[...]

    def set_visitors(k, at):
        va[at:at + VIS] = visitor_operand(unpack([vis_s[k, 0], vis_s[k, 1]]))
        vd[:, at:at + VIS] = unpack([vis_d[k, 0].astype(F32), vis_d[k, 1].astype(F32)]).astype(BF16)

    def pass_on(k):
        for which in range(2):
            z_copy(k, which).wait_recv()
        for which in range(2):
            sib_copy(k, which).start()
            if k + 2 <= HALF:
                z_copy(k + 2, which).start()

    def columns(g):
        return pl.ds(pl.multiple_of(g * CHUNK, CHUNK), CHUNK)

    for which in range(2):
        sib_copy(0, which).wait_recv()
    set_visitors(0, 0)

    def first(g, carry):
        for dy in range(NY):
            copy = home_copy(g, dy, g * NY + dy, 0)
            if dy:
                copy.wait_recv()
            else:
                pl.when(g > 0)(copy.wait_recv)
        cols = columns(g)
        hb[:, cols] = home_operand(unpack([home_s[g * NY + dy] for dy in range(NY)]))
        tile = matern(jnp.dot(va[0:VIS], hb[:, cols], preferred_element_type=F32))
        hacc[:, cols] += jnp.dot(vd[:, 0:VIS], tile, preferred_element_type=F32)

        @pl.when(g == 1)
        def _():
            pass_on(1)
            pass_on(2)

        return carry

    lax.fori_loop(0, NX, first, 0)
    for dx, dy in plane[1:]:
        home_copy(dx, dy, dx * NY + dy, 1).wait_recv()
    for g in range(NX):
        hd[:, columns(g)] = unpack([home_d[g * NY + dy].astype(F32) for dy in range(NY)]).astype(BF16)

    def cross_copy(k, part):
        pair, half = (k - 1) // 2, (k - 1) % 2
        src = ret.at[pair, :, pl.ds(VIS * half + 128, 128)] if part == 0 else ret_tail.at[k]
        dst = (cross_a, cross_b)[part].at[k]
        return remote(src, dst, cross_send.at[k, part], cross_recv.at[k, part], peer(dc=1))

    def fin_copy(k, part):
        src, dst = ((sum_head, fin_a), (sum_tail, fin_b))[part]
        return remote(src.at[k], dst.at[k], fin_send.at[k, part], fin_recv.at[k, part], peer(dz=k))

    def exchange(ks):
        for k in ks:
            pair, half = (k - 1) // 2, (k - 1) % 2
            ret_tail[k] = pack_high(ret[pair, :, pl.ds(VIS * half + 256, 128)])
            for part in range(2):
                cross_copy(k, part).start()

    def send_home(ks):
        for k in ks:
            pair, half = (k - 1) // 2, (k - 1) % 2
            for part in range(2):
                cross_copy(k, part).wait_recv()
            sum_head[k] = ret[pair, :, pl.ds(VIS * half, 128)] + cross_a[k]
            sum_tail[k] = pack_tail(ret[pair, :, pl.ds(VIS * half + 256, 128)]) + cross_b[k]
            for part in range(2):
                fin_copy(k, part).start()

    def visitors(k, at):
        for which in range(2):
            sib_copy(k, which).wait_recv()
        set_visitors(k, at)

    for pair in range(3):
        pass_on(2 * pair + 3)
        pass_on(2 * pair + 4)
        visitors(2 * pair + 1, 0)
        visitors(2 * pair + 2, VIS)

        def both(g, carry, pair=pair):
            cols = columns(g)
            tile = matern(jnp.dot(va[...], hb[:, cols], preferred_element_type=F32))
            hacc[:, cols] += jnp.dot(vd[...], tile, preferred_element_type=F32)
            ret[pair] += lax.dot_general(hd[:, cols], tile, NT, preferred_element_type=F32)
            if pair:
                pl.when(g == 1)(functools.partial(send_home, (2 * pair - 1, 2 * pair)))
            return carry

        lax.fori_loop(0, NX, both, 0)
        exchange((2 * pair + 1, 2 * pair + 2))

    visitors(7, 0)
    visitors(8, VIS)

    def seventh(g, carry):
        cols = columns(g)
        tile = matern(jnp.dot(va[0:VIS], hb[:, cols], preferred_element_type=F32))
        hacc[:, cols] += jnp.dot(vd[:, 0:VIS], tile, preferred_element_type=F32)
        ret[3, :, 0:VIS] += lax.dot_general(hd[:, cols], tile, NT, preferred_element_type=F32)
        pl.when(g == 1)(functools.partial(send_home, (5, 6)))
        return carry

    lax.fori_loop(0, NX, seventh, 0)
    exchange((7,))

    def red_copy(dx, dy, slot, part):
        base = dx * CHUNK + 128 * dy
        src = hacc.at[:, pl.ds(pl.multiple_of(base, 128), 128)] if part == 0 else red_tail.at[dx * NY + dy]
        dst = (red_a, red_b)[part].at[slot]
        return remote(src, dst, red_send.at[part, dx * NY + dy], red_recv.at[part, slot], peer(dx=dx, dy=dy))

    def back(dx, dy):
        return ((NX - dx) % NX) * NY + (NY - dy) % NY

    def eighth(t, carry):
        g = (t + 1) % NX
        cols = columns(g)
        tile = matern(jnp.dot(va[VIS:2 * VIS], hb[:, cols], preferred_element_type=F32))
        hacc[:, cols] += jnp.dot(vd[:, VIS:2 * VIS], tile, preferred_element_type=F32)
        for dy in range(NY):
            tails = hacc[:, pl.ds(pl.multiple_of(g * CHUNK + 512 + 128 * (dy // 2), 128), 128)]
            red_tail[g * NY + dy] = pack_high(tails) if dy % 2 else pack_tail(tails)

        def send(dy):
            for part in range(2):
                red_copy(g, dy, back(g, dy), part).start()

        for dy in range(1, NY):
            send(dy)
        pl.when(g > 0)(functools.partial(send, 0))
        pl.when(t == 1)(functools.partial(send_home, (7,)))
        return carry

    lax.fori_loop(0, NX, eighth, 0)

    fetches[3].wait()
    direction = dir_ref[...]
    residual = res_ref[...]
    sum_a, sum_b = hacc[:, 0:128], red_tail[0]
    for dx, dy in plane[1:]:
        for part in range(2):
            red_copy(dx, dy, dx * NY + dy, part).wait_recv()
        sum_a = sum_a + red_a[dx * NY + dy]
        sum_b = sum_b + red_b[dx * NY + dy]
    for k in range(1, HALF):
        for part in range(2):
            fin_copy(k, part).wait_recv()
        sum_a = sum_a + fin_a[k]
        sum_b = sum_b + fin_b[k]
    last_points = jnp.concatenate([sum_b, pltpu.roll(sum_b, 64, 1)], axis=0)[:, 0:64]
    kd = jnp.concatenate([sum_a, last_points], axis=1) + noise_ref[0] * direction
    kd_out[...] = kd

    def total(v):
        return jnp.sum(v, axis=1, keepdims=True)

    sums = to_row([total(residual * residual), total(direction * kd), total(residual * kd), total(kd * kd)])

    ar1_src[...] = jnp.broadcast_to(sums, (8, 128))
    me1 = x * NY + y

    def ar1_copy(dx, dy, slot):
        return remote(ar1_src, ar1.at[slot], ar1_send.at[dx * NY + dy], ar1_recv.at[slot], peer(dx=dx, dy=dy))

    for dx, dy in plane[1:]:
        ar1_copy(dx, dy, me1).start()
    ar1[me1] = ar1_src[...]
    for dx, dy in plane[1:]:
        ar1_copy(dx, dy, ((x + dx) % NX) * NY + (y + dy) % NY).wait_recv()
    acc = ar1[0]
    for i in range(1, NPEER):
        acc = acc + ar1[i]
    ar2_src[...] = acc

    def ar2_copy(dz, slot):
        return remote(ar2_src, ar2.at[slot], ar2_send.at[dz], ar2_recv.at[slot], peer(dz=dz))

    for dz in range(1, NZ):
        ar2_copy(dz, z).start()
    ar2[z] = acc
    for dz in range(1, NZ):
        ar2_copy(dz, (z + dz) % NZ).wait_recv()
    acc = ar2[0]
    for i in range(1, NZ):
        acc = acc + ar2[i]
    ar3_src[...] = acc
    last = remote(ar3_src, ar3, ar3_send, ar3_recv, peer(dc=1))
    last.start()
    last.wait_recv()
    acc = (ar3_src[...] + ar3[...])[0:1]

    rr, curve, r_kd, kd_sq = (to_col(acc, i) for i in range(4))
    alpha = rr / curve
    norm_sq = rr - 2.0 * alpha * r_kd + alpha * alpha * kd_sq
    lane = lax.broadcasted_iota(jnp.int32, (32, 128), 1)
    coef_out[...] = jnp.where(lane == 0, alpha, jnp.where(lane == 1, norm_sq / rr, norm_sq))

    for which in range(2):
        for pos in range(HALF + 1):
            if pos:
                z_copy(pos, which).wait_send()
            sib_copy(pos, which).wait_send()
        for dx, dy in plane[1:]:
            home_copy(dx, dy, dx * NY + dy, which).wait_send()
            red_copy(dx, dy, dx * NY + dy, which).wait_send()
    for k in range(1, HALF):
        for part in range(2):
            cross_copy(k, part).wait_send()
            fin_copy(k, part).wait_send()
    for dx, dy in plane[1:]:
        ar1_copy(dx, dy, me1).wait_send()
    for dz in range(1, NZ):
        ar2_copy(dz, z).wait_send()
    last.wait_send()


def body(points, lengthscale, noise, direction, residual, solution):
    vmem, smem = pl.BlockSpec(memory_space=pltpu.VMEM), pl.BlockSpec(memory_space=pltpu.SMEM)
    hbm = pl.BlockSpec(memory_space=pl.ANY)
    dma = pltpu.SemaphoreType.DMA
    kd, coef = pl.pallas_call(
        kernel,
        out_shape=[jax.ShapeDtypeStruct((32, BLK), F32), jax.ShapeDtypeStruct((32, 128), F32)],
        in_specs=[hbm, hbm, smem, hbm, hbm],
        out_specs=[vmem] * 2,
        scratch_shapes=[
            pltpu.VMEM((32, BLK), F32),
            pltpu.VMEM((1, 32), F32),
            pltpu.VMEM((32, BLK), F32),
            pltpu.VMEM((32, BLK), F32),
            pltpu.VMEM((32, 128), F32),
            pltpu.VMEM((48, 128), F32),
            pltpu.VMEM((48, 128), BF16),
            pltpu.VMEM((NPEER, 48, 128), F32),
            pltpu.VMEM((NPEER, 48, 128), BF16),
            pltpu.VMEM((HALF + 1, 2, 48, 128), F32),
            pltpu.VMEM((HALF + 1, 2, 48, 128), BF16),
            pltpu.VMEM((256, HOME), BF16),
            pltpu.VMEM((32, HOME), BF16),
            pltpu.VMEM((2 * VIS, 256), BF16),
            pltpu.VMEM((32, 2 * VIS), BF16),
            pltpu.VMEM((32, HOME), F32),
            pltpu.VMEM((HALF // 2, 32, 2 * VIS), F32),
            pltpu.VMEM((HALF, 16, 128), F32),
            pltpu.VMEM((HALF, 32, 128), F32),
            pltpu.VMEM((HALF, 16, 128), F32),
            pltpu.VMEM((NPEER, 16, 128), F32),
            pltpu.VMEM((HALF, 32, 128), F32),
            pltpu.VMEM((HALF, 16, 128), F32),
            pltpu.VMEM((HALF, 32, 128), F32),
            pltpu.VMEM((HALF, 16, 128), F32),
            pltpu.VMEM((NPEER, 32, 128), F32),
            pltpu.VMEM((NPEER, 16, 128), F32),
            pltpu.VMEM((8, 128), F32),
            pltpu.VMEM((NPEER, 8, 128), F32),
            pltpu.VMEM((8, 128), F32),
            pltpu.VMEM((NZ, 8, 128), F32),
            pltpu.VMEM((8, 128), F32),
            pltpu.VMEM((8, 128), F32),
            dma((4,)),
            dma((2, NPEER)), dma((2, NPEER)),
            dma((2, HALF + 1)), dma((2, HALF + 1)),
            dma((2, HALF + 1)), dma((2, HALF + 1)),
            dma((HALF, 2)), dma((HALF, 2)),
            dma((HALF, 2)), dma((HALF, 2)),
            dma((2, NPEER)), dma((2, NPEER)),
            dma((NPEER,)), dma((NPEER,)),
            dma((NZ,)), dma((NZ,)),
            dma, dma,
        ],
        compiler_params=pltpu.CompilerParams(
            collective_id=0, has_side_effects=True, vmem_limit_bytes=63 * 1024 * 1024
        ),
    )(points, lengthscale.reshape(1, 32), noise, direction, residual)
    alpha, beta = coef[:, 0:1], coef[:, 1:2]
    new_residual = residual - alpha * kd
    return (solution + alpha * direction, new_residual, new_residual + beta * direction, coef[:, 2])


def solution(mesh):
    data = P(None, ("wide", "narrow"))
    return jax.shard_map(
        body,
        mesh=mesh,
        in_specs=(data, P(), P(), data, data, data),
        out_specs=(data, data, data, P()),
        check_vma=False,
    )
```

time: 92.8 us -> 83 us (0.89)
  Pallas kernels: 85.1 us -> 78.3 us
  local copies, waits for them, and re-layouts: 6.03 us -> 1.55 us
  other arithmetic: 0 us -> 1.47 us
    pallas_call x1, Pallas kernels: 85.1 us -> 78.3 us  [body(): pl.pallas_call(kernel, out_shape=[jax.ShapeDtypeStruct((32, BLK), F32), j...]
    unnamed x14 -> x6, local copies, waits for them, and re-layouts: 6.03 us -> 0.01 us
    slice x0 -> x1, local copies, waits for them, and re-layouts: none -> 1.53 us  [body(): coef[:, 2]]
    add x0 -> x1, other arithmetic: none -> 1.47 us  [body(): new_residual + beta * direction]
where the time goes in v2:
time: 83 us; the launch traced here: 82.7 us
  Pallas kernels  78.3 us (94%)
  local copies, waits for them, and re-layouts  1.55 us (2%)
  other arithmetic  1.47 us (2%)
  between operations  1.31 us (2%)
    pallas_call x1, Pallas kernels, body(): pl.pallas_call(kernel, out_shape=[jax.ShapeDtypeStruct((32, BLK), F32), j...  78.3 us

profile of v2, /device:TPU:1, one launch (start us, length us, event | category | flops | bytes accessed | tf_op | source)
XLA Modules:
  0.0 82.7 jit_solution(9131014735436749291)
XLA Ops:
  1.3 0.0 copy-start.1
  1.3 0.0 copy-start.2
  1.3 78.3 %shard_map.93 = (f32[32,192]{1,0:T(8,128)}, f32[32,128]{1,0:T(8,128)}) custom-call(f32[32,192]{1,0:T(8,128)} %pts_hbm.1, f32[1,32]{1,0:T(1,128)} %bitcast.1, f32[1]{0:T(128)S(6)} %copy.10.noise_ref, f32[32,192]{1,0:T(8,128)} %dir_hbm.1, f32[32,192]{1,0:T(8,128)} %res_hbm.1), custom_call_target="tpu_custom_call" | custom-call | tf_op jit(solution)/shard_map/pallas_call | solution.py:410
  79.6 0.0 copy-start
  79.6 1.5 %slice_reduce_fusion = (f32[32]{0:T(128)}, f32[32]{0:T(128)S(1)}, f32[32]{0:T(128)S(1)}) fusion(f32[32,128]{1,0:T(8,128)} %get-tuple-element.6), kind=kLoop, calls=%fused_computation.3 | loop fusion | bytes 768 | tf_op jit(solution)/shard_map/slice | solution.py:466
  81.2 0.0 copy-done.1
  81.2 0.0 copy-done.2
  81.2 0.0 copy-done
  81.2 1.5 %multiply_add_fusion = (f32[32,192]{1,0:T(8,128)}, f32[32,192]{1,0:T(8,128)}, f32[32,192]{1,0:T(8,128)}) fusion(f32[32,192]{1,0:T(8,128)S(1)} %copy-done, f32[32]{0:T(128)S(1)} %get-tuple-element.9, f32[32,192]{1,0:T(8,128)S(1)} %copy-done.1, f32[32,192]{1,0:T(8,128)} %get-tuple-element.7, f32[32]{0:T(128)S(1)} %get-tuple-element.10, f32[32,192]{1,0:T(8,128)S(1)} %copy-done.2), kind=kLoop, calls=%fused_computation | loop fusion | flops 36864 | bytes 172288 | tf_op jit(solution)/shard_map/add | solution.py:466
Async XLA Ops:
  1.3 79.9 %copy-start.1 = (f32[32,192]{1,0:T(8,128)S(1)}, f32[32,192]{1,0:T(8,128)}, u32[]{:S(2)}) copy-start(f32[32,192]{1,0:T(8,128)} %res_hbm.1) | copy-start | bytes 73732
  1.3 79.9 %copy-start.2 = (f32[32,192]{1,0:T(8,128)S(1)}, f32[32,192]{1,0:T(8,128)}, u32[]{:S(2)}) copy-start(f32[32,192]{1,0:T(8,128)} %param.11) | copy-start | bytes 73732
  79.6 1.6 %copy-start = (f32[32,192]{1,0:T(8,128)S(1)}, f32[32,192]{1,0:T(8,128)}, u32[]{:S(2)}) copy-start(f32[32,192]{1,0:T(8,128)} %dir_hbm.1) | copy-start | bytes 73732

commit v3 on v2

--- a/solution.py
+++ b/solution.py
@@ -100,12 +100,12 @@
 
 def kernel(
     pts_hbm, ls_hbm, noise_ref, dir_hbm, res_hbm,
-    kd_out, coef_out,
+    kd_out, alpha_out, beta_out, norm_out,
     pts_ref, ls_ref, dir_ref, res_ref,
     tail, own_s, own_d, home_s, home_d, vis_s, vis_d, hb, hd, va, vd, hacc, ret, ret_tail, sum_head, sum_tail, red_tail,
-    cross_a, cross_b, fin_a, fin_b, red_a, red_b, ar1_src, ar1, ar2_src, ar2, ar3_src, ar3,
+    cross_a, cross_b, fin_a, fin_b, red_a, red_b, ar1_src, ar1, ar2_src, ar2,
     in_sem, home_send, home_recv, zs_send, z_recv, sib_send, sib_recv,
-    cross_send, cross_recv, fin_send, fin_recv, red_send, red_recv, ar1_send, ar1_recv, ar2_send, ar2_recv, ar3_send, ar3_recv,
+    cross_send, cross_recv, fin_send, fin_recv, red_send, red_recv, ar1_send, ar1_recv, ar2_send, ar2_recv,
 ):
     wide, narrow = lax.axis_index("wide"), lax.axis_index("narrow")
     z, y_hi, core = wide // 4, (wide // 2) % 2, wide % 2
@@ -167,17 +167,16 @@
         src = own[which] if k == 0 else vis[which].at[k, 0]
         return remote(src, vis[which].at[k, 1], sib_send.at[which, k], sib_recv.at[which, k], peer(dc=1))
 
-    def home_start(which):
-        for dx, dy in plane[1:]:
-            home_copy(dx, dy, ((-dx) % NX) * NY + (-dy) % NY, which).start()
-
     for which in range(2):
         sib_copy(0, which).start()
     for k in (1, 2):
         for which in range(2):
             z_copy(k, which).start()
-    home_start(0)
-    home_start(1)
+    for dx in (0, 1, 3, 2):
+        for dy in range(NY):
+            if dx or dy:
+                for which in range(2):
+                    home_copy(dx, dy, ((-dx) % NX) * NY + (-dy) % NY, which).start()
 
     vis_s[0, 0] = own_s[...]
     vis_d[0, 0] = own_d[...]
@@ -199,34 +198,42 @@
     def columns(g):
         return pl.ds(pl.multiple_of(g * CHUNK, CHUNK), CHUNK)
 
-    for which in range(2):
-        sib_copy(0, which).wait_recv()
-    set_visitors(0, 0)
-
-    def first(g, carry):
+    def visitors(k, at):
+        for which in range(2):
+            sib_copy(k, which).wait_recv()
+        set_visitors(k, at)
+
+    def begin():
+        for k in (1, 2):
+            pass_on(k)
+        for k in (1, 2):
+            visitors(k, VIS * (k - 1))
+
+    def first(t, carry):
+        g = t + (t // 2) * (5 - 2 * t)
         for dy in range(NY):
-            copy = home_copy(g, dy, g * NY + dy, 0)
-            if dy:
-                copy.wait_recv()
-            else:
-                pl.when(g > 0)(copy.wait_recv)
+            for which in range(2):
+                copy = home_copy(g, dy, g * NY + dy, which)
+                if dy:
+                    copy.wait_recv()
+                else:
+                    pl.when(t > 0)(copy.wait_recv)
         cols = columns(g)
         hb[:, cols] = home_operand(unpack([home_s[g * NY + dy] for dy in range(NY)]))
-        tile = matern(jnp.dot(va[0:VIS], hb[:, cols], preferred_element_type=F32))
-        hacc[:, cols] += jnp.dot(vd[:, 0:VIS], tile, preferred_element_type=F32)
-
-        @pl.when(g == 1)
+        hd[:, cols] = unpack([home_d[g * NY + dy].astype(F32) for dy in range(NY)]).astype(BF16)
+        pl.when(t == 0)(begin)
+
+        @pl.when(t == 2)
         def _():
-            pass_on(1)
-            pass_on(2)
-
+            pass_on(3)
+            pass_on(4)
+
+        tile = matern(jnp.dot(va[...], hb[:, cols], preferred_element_type=F32))
+        hacc[:, cols] += jnp.dot(vd[...], tile, preferred_element_type=F32)
+        ret[0] += lax.dot_general(hd[:, cols], tile, NT, preferred_element_type=F32)
         return carry
 
     lax.fori_loop(0, NX, first, 0)
-    for dx, dy in plane[1:]:
-        home_copy(dx, dy, dx * NY + dy, 1).wait_recv()
-    for g in range(NX):
-        hd[:, columns(g)] = unpack([home_d[g * NY + dy].astype(F32) for dy in range(NY)]).astype(BF16)
 
     def cross_copy(k, part):
         pair, half = (k - 1) // 2, (k - 1) % 2
@@ -255,14 +262,9 @@
             for part in range(2):
                 fin_copy(k, part).start()
 
-    def visitors(k, at):
-        for which in range(2):
-            sib_copy(k, which).wait_recv()
-        set_visitors(k, at)
-
-    for pair in range(3):
-        pass_on(2 * pair + 3)
-        pass_on(2 * pair + 4)
+    exchange((1, 2))
+
+    for pair in (1, 2):
         visitors(2 * pair + 1, 0)
         visitors(2 * pair + 2, VIS)
 
@@ -271,15 +273,19 @@
             tile = matern(jnp.dot(va[...], hb[:, cols], preferred_element_type=F32))
             hacc[:, cols] += jnp.dot(vd[...], tile, preferred_element_type=F32)
             ret[pair] += lax.dot_general(hd[:, cols], tile, NT, preferred_element_type=F32)
-            if pair:
-                pl.when(g == 1)(functools.partial(send_home, (2 * pair - 1, 2 * pair)))
+
+            @pl.when(g == 1)
+            def _():
+                pass_on(2 * pair + 3)
+                pass_on(2 * pair + 4)
+                send_home((2 * pair - 1, 2 * pair))
+
             return carry
 
         lax.fori_loop(0, NX, both, 0)
         exchange((2 * pair + 1, 2 * pair + 2))
 
     visitors(7, 0)
-    visitors(8, VIS)
 
     def seventh(g, carry):
         cols = columns(g)
@@ -292,6 +298,8 @@
     lax.fori_loop(0, NX, seventh, 0)
     exchange((7,))
 
+    visitors(8, 0)
+    visitors(0, VIS)
     def red_copy(dx, dy, slot, part):
         base = dx * CHUNK + 128 * dy
         src = hacc.at[:, pl.ds(pl.multiple_of(base, 128), 128)] if part == 0 else red_tail.at[dx * NY + dy]
@@ -301,11 +309,11 @@
     def back(dx, dy):
         return ((NX - dx) % NX) * NY + (NY - dy) % NY
 
-    def eighth(t, carry):
+    def last_pair(t, carry):
         g = (t + 1) % NX
         cols = columns(g)
-        tile = matern(jnp.dot(va[VIS:2 * VIS], hb[:, cols], preferred_element_type=F32))
-        hacc[:, cols] += jnp.dot(vd[:, VIS:2 * VIS], tile, preferred_element_type=F32)
+        tile = matern(jnp.dot(va[...], hb[:, cols], preferred_element_type=F32))
+        hacc[:, cols] += jnp.dot(vd[...], tile, preferred_element_type=F32)
         for dy in range(NY):
             tails = hacc[:, pl.ds(pl.multiple_of(g * CHUNK + 512 + 128 * (dy // 2), 128), 128)]
             red_tail[g * NY + dy] = pack_high(tails) if dy % 2 else pack_tail(tails)
@@ -317,10 +325,10 @@
         for dy in range(1, NY):
             send(dy)
         pl.when(g > 0)(functools.partial(send, 0))
-        pl.when(t == 1)(functools.partial(send_home, (7,)))
+        pl.when(t == 0)(functools.partial(send_home, (7,)))
         return carry
 
-    lax.fori_loop(0, NX, eighth, 0)
+    lax.fori_loop(0, NX, last_pair, 0)
 
     fetches[3].wait()
     direction = dir_ref[...]
@@ -345,45 +353,17 @@
 
     sums = to_row([total(residual * residual), total(direction * kd), total(residual * kd), total(kd * kd)])
 
-    ar1_src[...] = jnp.broadcast_to(sums, (8, 128))
-    me1 = x * NY + y
-
-    def ar1_copy(dx, dy, slot):
-        return remote(ar1_src, ar1.at[slot], ar1_send.at[dx * NY + dy], ar1_recv.at[slot], peer(dx=dx, dy=dy))
-
-    for dx, dy in plane[1:]:
-        ar1_copy(dx, dy, me1).start()
-    ar1[me1] = ar1_src[...]
-    for dx, dy in plane[1:]:
-        ar1_copy(dx, dy, ((x + dx) % NX) * NY + (y + dy) % NY).wait_recv()
-    acc = ar1[0]
-    for i in range(1, NPEER):
-        acc = acc + ar1[i]
-    ar2_src[...] = acc
-
-    def ar2_copy(dz, slot):
-        return remote(ar2_src, ar2.at[slot], ar2_send.at[dz], ar2_recv.at[slot], peer(dz=dz))
-
-    for dz in range(1, NZ):
-        ar2_copy(dz, z).start()
-    ar2[z] = acc
-    for dz in range(1, NZ):
-        ar2_copy(dz, (z + dz) % NZ).wait_recv()
-    acc = ar2[0]
-    for i in range(1, NZ):
-        acc = acc + ar2[i]
-    ar3_src[...] = acc
-    last = remote(ar3_src, ar3, ar3_send, ar3_recv, peer(dc=1))
-    last.start()
-    last.wait_recv()
-    acc = (ar3_src[...] + ar3[...])[0:1]
-
-    rr, curve, r_kd, kd_sq = (to_col(acc, i) for i in range(4))
-    alpha = rr / curve
-    norm_sq = rr - 2.0 * alpha * r_kd + alpha * alpha * kd_sq
-    lane = lax.broadcasted_iota(jnp.int32, (32, 128), 1)
-    coef_out[...] = jnp.where(lane == 0, alpha, jnp.where(lane == 1, norm_sq / rr, norm_sq))
-
+    ar1_src[...] = sums
+    me1 = (x * NY + y) * 2 + core
+    near = [(dx, dy, dc) for dx, dy in plane for dc in range(2)][1:]
+
+    def ar1_copy(dx, dy, dc, slot):
+        i = (dx * NY + dy) * 2 + dc
+        return remote(ar1_src, ar1.at[slot], ar1_send.at[i], ar1_recv.at[slot], peer(dx=dx, dy=dy, dc=dc))
+
+    for dx, dy, dc in near:
+        ar1_copy(dx, dy, dc, me1).start()
+    ar1[me1] = sums
     for which in range(2):
         for pos in range(HALF + 1):
             if pos:
@@ -396,22 +376,44 @@
         for part in range(2):
             cross_copy(k, part).wait_send()
             fin_copy(k, part).wait_send()
-    for dx, dy in plane[1:]:
-        ar1_copy(dx, dy, me1).wait_send()
+    for dx, dy, dc in near:
+        ar1_copy(dx, dy, dc, (((x + dx) % NX) * NY + (y + dy) % NY) * 2 + (core + dc) % 2).wait_recv()
+    acc = jnp.sum(ar1[...], axis=0)
+    ar2_src[...] = acc
+
+    def ar2_copy(dz, slot):
+        return remote(ar2_src, ar2.at[slot], ar2_send.at[dz], ar2_recv.at[slot], peer(dz=dz))
+
+    for dz in range(1, NZ):
+        ar2_copy(dz, z).start()
+    ar2[z] = acc
+    for dz in range(1, NZ):
+        ar2_copy(dz, (z + dz) % NZ).wait_recv()
+    acc = jnp.sum(ar2[...], axis=0)
+
+    rr, curve, r_kd, kd_sq = (to_col(acc, i) for i in range(4))
+    alpha = rr / curve
+    norm_sq = rr - 2.0 * alpha * r_kd + alpha * alpha * kd_sq
+    alpha_out[...] = jnp.broadcast_to(alpha, (32, BLK))
+    beta_out[...] = jnp.broadcast_to(norm_sq / rr, (32, BLK))
+    norm_out[...] = jnp.sum(jnp.where(eye, norm_sq, 0.0), axis=0, keepdims=True)
+
+    for dx, dy, dc in near:
+        ar1_copy(dx, dy, dc, me1).wait_send()
     for dz in range(1, NZ):
         ar2_copy(dz, z).wait_send()
-    last.wait_send()
 
 
 def body(points, lengthscale, noise, direction, residual, solution):
     vmem, smem = pl.BlockSpec(memory_space=pltpu.VMEM), pl.BlockSpec(memory_space=pltpu.SMEM)
     hbm = pl.BlockSpec(memory_space=pl.ANY)
     dma = pltpu.SemaphoreType.DMA
-    kd, coef = pl.pallas_call(
+    block = jax.ShapeDtypeStruct((32, BLK), F32)
+    kd, alpha, beta, norm_sq = pl.pallas_call(
         kernel,
-        out_shape=[jax.ShapeDtypeStruct((32, BLK), F32), jax.ShapeDtypeStruct((32, 128), F32)],
+        out_shape=[block, block, block, jax.ShapeDtypeStruct((1, 32), F32)],
         in_specs=[hbm, hbm, smem, hbm, hbm],
-        out_specs=[vmem] * 2,
+        out_specs=[vmem] * 4,
         scratch_shapes=[
             pltpu.VMEM((32, BLK), F32),
             pltpu.VMEM((1, 32), F32),
@@ -440,12 +442,10 @@
             pltpu.VMEM((HALF, 16, 128), F32),
             pltpu.VMEM((NPEER, 32, 128), F32),
             pltpu.VMEM((NPEER, 16, 128), F32),
-            pltpu.VMEM((8, 128), F32),
-            pltpu.VMEM((NPEER, 8, 128), F32),
-            pltpu.VMEM((8, 128), F32),
-            pltpu.VMEM((NZ, 8, 128), F32),
-            pltpu.VMEM((8, 128), F32),
-            pltpu.VMEM((8, 128), F32),
+            pltpu.VMEM((1, 128), F32),
+            pltpu.VMEM((2 * NPEER, 1, 128), F32),
+            pltpu.VMEM((1, 128), F32),
+            pltpu.VMEM((NZ, 1, 128), F32),
             dma((4,)),
             dma((2, NPEER)), dma((2, NPEER)),
             dma((2, HALF + 1)), dma((2, HALF + 1)),
@@ -453,17 +453,15 @@
             dma((HALF, 2)), dma((HALF, 2)),
             dma((HALF, 2)), dma((HALF, 2)),
             dma((2, NPEER)), dma((2, NPEER)),
-            dma((NPEER,)), dma((NPEER,)),
+            dma((2 * NPEER,)), dma((2 * NPEER,)),
             dma((NZ,)), dma((NZ,)),
-            dma, dma,
         ],
         compiler_params=pltpu.CompilerParams(
             collective_id=0, has_side_effects=True, vmem_limit_bytes=63 * 1024 * 1024
         ),
     )(points, lengthscale.reshape(1, 32), noise, direction, residual)
-    alpha, beta = coef[:, 0:1], coef[:, 1:2]
     new_residual = residual - alpha * kd
-    return (solution + alpha * direction, new_residual, new_residual + beta * direction, coef[:, 2])
+    return (solution + alpha * direction, new_residual, new_residual + beta * direction, norm_sq.reshape(32))
 
 
 def solution(mesh):

time: 83 us -> 75.6 us (0.911)
  Pallas kernels: 78.3 us -> 71.3 us
    pallas_call x1, Pallas kernels: 78.3 us -> 71.3 us  [body(): pl.pallas_call(kernel, out_shape=[block, block, block, jax.ShapeDtypeStru...]
    slice x1 -> x0, local copies, waits for them, and re-layouts: 1.53 us -> none  [body(): coef[:, 2]]
    unnamed x6 -> x9, local copies, waits for them, and re-layouts: 0.01 us -> 1.19 us
where the time goes in v3:
time: 75.6 us; the launch traced here: 75.3 us
  Pallas kernels  71.3 us (94%)
  other arithmetic  1.44 us (2%)
  between operations  1.33 us (2%)
  local copies, waits for them, and re-layouts  1.19 us (2%)
    pallas_call x1, Pallas kernels, body(): pl.pallas_call(kernel, out_shape=[block, block, block, jax.ShapeDtypeStru...  71.3 us

profile of v3, /device:TPU:1, one launch (start us, length us, event | category | flops | bytes accessed | tf_op | source)
XLA Modules:
  0.0 75.3 jit_solution(10172096515744965614)
XLA Ops:
  1.3 0.0 copy-start
  1.3 0.0 copy-start.1
  1.3 0.0 copy-start.2
  1.3 71.3 %shard_map.93 = (f32[32,192]{1,0:T(8,128)}, f32[32,192]{1,0:T(8,128)}, f32[32,192]{1,0:T(8,128)}, f32[1,32]{1,0:T(1,128)}) custom-call(f32[32,192]{1,0:T(8,128)} %pts_hbm.1, f32[1,32]{1,0:T(1,128)} %bitcast.2, f32[1]{0:T(128)S(6)} %copy.11.noise_ref, f32[32,192]{1,0:T(8,128)} %dir_hbm.1, f32[32,192]{1,0:T(8,128)} %res_hbm.1), custom_call_target="tpu_custom_call" | custom-call | tf_op jit(solution)/shard_map/pallas_call | solution.py:412
  72.7 0.0 copy-done
  72.7 0.0 copy-done.1
  72.7 0.0 copy-done.2
  72.7 1.4 %multiply_add_fusion = (f32[32,192]{1,0:T(8,128)}, f32[32,192]{1,0:T(8,128)}, f32[32,192]{1,0:T(8,128)}) fusion(f32[32,192]{1,0:T(8,128)} %get-tuple-element.10, f32[32,192]{1,0:T(8,128)S(1)} %copy-done, f32[32,192]{1,0:T(8,128)S(1)} %copy-done.1, f32[32,192]{1,0:T(8,128)} %get-tuple-element.8, f32[32,192]{1,0:T(8,128)} %get-tuple-element.9, ...), kind=kLoop, calls=%fused_computation | loop fusion | flops 36864 | bytes 221184 | tf_op jit(solution)/shard_map/add | solution.py:464
  74.1 0.0 copy-start.3
  74.1 0.7 copy-done.3
  74.8 0.5 copy.12
Async XLA Ops:
  1.3 71.4 %copy-start = (f32[32,192]{1,0:T(8,128)S(1)}, f32[32,192]{1,0:T(8,128)}, u32[]{:S(2)}) copy-start(f32[32,192]{1,0:T(8,128)} %dir_hbm.1) | copy-start | bytes 73732
  1.3 71.4 %copy-start.1 = (f32[32,192]{1,0:T(8,128)S(1)}, f32[32,192]{1,0:T(8,128)}, u32[]{:S(2)}) copy-start(f32[32,192]{1,0:T(8,128)} %res_hbm.1) | copy-start | bytes 73732
  1.3 71.4 %copy-start.2 = (f32[32,192]{1,0:T(8,128)S(1)}, f32[32,192]{1,0:T(8,128)}, u32[]{:S(2)}) copy-start(f32[32,192]{1,0:T(8,128)} %param.11) | copy-start | bytes 73732
  74.1 0.7 copy-start.3

commit v4 on v3

--- a/solution.py
+++ b/solution.py
@@ -100,7 +100,7 @@
 
 def kernel(
     pts_hbm, ls_hbm, noise_ref, dir_hbm, res_hbm,
-    kd_out, alpha_out, beta_out, norm_out,
+    kd_out, alpha_out, beta_out, ratio_out, rr_out,
     pts_ref, ls_ref, dir_ref, res_ref,
     tail, own_s, own_d, home_s, home_d, vis_s, vis_d, hb, hd, va, vd, hacc, ret, ret_tail, sum_head, sum_tail, red_tail,
     cross_a, cross_b, fin_a, fin_b, red_a, red_b, ar1_src, ar1, ar2_src, ar2,
@@ -396,7 +396,8 @@
     norm_sq = rr - 2.0 * alpha * r_kd + alpha * alpha * kd_sq
     alpha_out[...] = jnp.broadcast_to(alpha, (32, BLK))
     beta_out[...] = jnp.broadcast_to(norm_sq / rr, (32, BLK))
-    norm_out[...] = jnp.sum(jnp.where(eye, norm_sq, 0.0), axis=0, keepdims=True)
+    ratio_out[...] = jnp.sum(jnp.where(eye, norm_sq / rr, 0.0), axis=0)
+    rr_out[...] = jnp.sum(jnp.where(eye, rr, 0.0), axis=0)
 
     for dx, dy, dc in near:
         ar1_copy(dx, dy, dc, me1).wait_send()
@@ -409,11 +410,12 @@
     hbm = pl.BlockSpec(memory_space=pl.ANY)
     dma = pltpu.SemaphoreType.DMA
     block = jax.ShapeDtypeStruct((32, BLK), F32)
-    kd, alpha, beta, norm_sq = pl.pallas_call(
+    row = jax.ShapeDtypeStruct((32,), F32)
+    kd, alpha, beta, ratio, rr = pl.pallas_call(
         kernel,
-        out_shape=[block, block, block, jax.ShapeDtypeStruct((1, 32), F32)],
+        out_shape=[block, block, block, row, row],
         in_specs=[hbm, hbm, smem, hbm, hbm],
-        out_specs=[vmem] * 4,
+        out_specs=[vmem] * 5,
         scratch_shapes=[
             pltpu.VMEM((32, BLK), F32),
             pltpu.VMEM((1, 32), F32),
@@ -461,7 +463,7 @@
         ),
     )(points, lengthscale.reshape(1, 32), noise, direction, residual)
     new_residual = residual - alpha * kd
-    return (solution + alpha * direction, new_residual, new_residual + beta * direction, norm_sq.reshape(32))
+    return (solution + alpha * direction, new_residual, new_residual + beta * direction, ratio * rr)
 
 
 def solution(mesh):

time: 75.6 us -> 75.7 us (level)
  no operation moved by 1% of the time
where the time goes in v4:
time: 75.7 us; the launch traced here: 75.4 us
  Pallas kernels  71.5 us (94%)
  other arithmetic  1.95 us (3%)
  between operations  1.34 us (2%)
    pallas_call x1, Pallas kernels, body(): pl.pallas_call(kernel, out_shape=[block, block, block, row, row], in_spec...  71.5 us

profile of v4, /device:TPU:1, one launch (start us, length us, event | category | flops | bytes accessed | tf_op | source)
XLA Modules:
  0.0 75.4 jit_solution(17254514562948190301)
XLA Ops:
  1.3 0.0 copy-start
  1.3 0.0 copy-start.1
  1.3 0.0 copy-start.2
  1.3 71.5 %shard_map.93 = (f32[32,192]{1,0:T(8,128)}, f32[32,192]{1,0:T(8,128)}, f32[32,192]{1,0:T(8,128)}, f32[32]{0:T(128)}, f32[32]{0:T(128)}) custom-call(f32[32,192]{1,0:T(8,128)} %pts_hbm.1, f32[1,32]{1,0:T(1,128)} %bitcast.1, f32[1]{0:T(128)S(6)} %copy.10.noise_ref, f32[32,192]{1,0:T(8,128)} %dir_hbm.1, f32[32,192]{1,0:T(8,128)} %res_hbm.1), custom_call_target="tpu_custom_call" | custom-call | tf_op jit(solution)/shard_map/pallas_call | solution.py:414
  72.8 0.0 copy-done
  72.8 0.0 copy-done.1
  72.8 0.0 copy-done.2
  72.8 1.4 %multiply_add_fusion = (f32[32,192]{1,0:T(8,128)}, f32[32,192]{1,0:T(8,128)}, f32[32,192]{1,0:T(8,128)}) fusion(f32[32,192]{1,0:T(8,128)} %get-tuple-element.11, f32[32,192]{1,0:T(8,128)S(1)} %copy-done, f32[32,192]{1,0:T(8,128)S(1)} %copy-done.1, f32[32,192]{1,0:T(8,128)} %get-tuple-element.9, f32[32,192]{1,0:T(8,128)} %get-tuple-element.10, ...), kind=kLoop, calls=%fused_computation | loop fusion | flops 36864 | bytes 221184 | tf_op jit(solution)/shard_map/add | solution.py:466
  74.2 0.0 copy-start.3
  74.2 0.0 copy-start.4
  74.2 0.6 copy-done.3
  74.9 0.0 copy-done.4
  74.9 0.5 mul.15
Async XLA Ops:
  1.3 71.5 %copy-start = (f32[32,192]{1,0:T(8,128)S(1)}, f32[32,192]{1,0:T(8,128)}, u32[]{:S(2)}) copy-start(f32[32,192]{1,0:T(8,128)} %dir_hbm.1) | copy-start | bytes 73732
  1.3 71.5 %copy-start.1 = (f32[32,192]{1,0:T(8,128)S(1)}, f32[32,192]{1,0:T(8,128)}, u32[]{:S(2)}) copy-start(f32[32,192]{1,0:T(8,128)} %res_hbm.1) | copy-start | bytes 73732
  1.3 71.5 %copy-start.2 = (f32[32,192]{1,0:T(8,128)S(1)}, f32[32,192]{1,0:T(8,128)}, u32[]{:S(2)}) copy-start(f32[32,192]{1,0:T(8,128)} %param.11) | copy-start | bytes 73732
  74.2 0.6 copy-start.3
  74.2 0.6 copy-start.4
